TPU v7x, 128 devices: a whole 4x4x4 slice. The times are simulated.
128 devices in a mesh: row: 4 (over x), col: 16 (over y, z_lo, core), dp: 2 (over z_hi).
Axes of the slice: x: 4, y: 4, z: 4 (z_hi: 2, z_lo: 2; z = z_hi * 2 + z_lo), core: 2. Of those that a mesh axis runs over, the one named last changes fastest.
Arguments:
- gradients: bfloat16 [2, 2560, 14336], P('dp', 'row', 'col'), may hold values from -6 to 6
- left_basis: bfloat16 [2560, 2560], P('col', 'row'), may hold values from -0.125 to 0.125
- right_basis: bfloat16 [14336, 14336], P('col', ('row', 'dp')), may hold values from -0.046875 to 0.046875
- first_moment: float32 [2560, 14336], P('col', ('row', 'dp')), may hold values from -1.8 to 1.8
- second_moment: float32 [2560, 14336], P('col', ('row', 'dp')), may hold values from 0.02 to 0.5
- omega_left: bfloat16 [2560, 128], replicated, may hold values from -0.125 to 0.125
- omega_right: bfloat16 [14336, 128], P('col'), may hold values from -0.046875 to 0.046875
- sketch_left: float32 [2560, 128], P(('row', 'col', 'dp')), may hold values from -6 to 6
- sketch_right: float32 [14336, 128], P('col'), may hold values from -6 to 6
Outputs:
- update: bfloat16 [2560, 14336], P(('row', 'dp'), 'col')
- first_new: float32 [2560, 14336], P('col', ('row', 'dp'))
- second_new: float32 [2560, 14336], P('col', ('row', 'dp'))
- left_new: float32 [2560, 128], P(('row', 'col', 'dp'))
- right_new: float32 [14336, 128], P('col')
All inputs are finite; a program needn't handle non-finite values.
Results may differ from a plain program's by a relative error of at most 0.027.
Values may be sent and summed in bfloat16 or wider, within the bound.
No kernel may reach another device: no remote copies, remote signals or barrier semaphores. Data moves between devices by JAX's collectives and lax.ppermute only.
A program may use at most 128 MiB of HBM per device.

v0:
```python
import math

import jax
import jax.numpy as jnp
from jax import lax
from jax.sharding import PartitionSpec as P

D = 2560
F = 14336


def on_device(
    gradients,
    left_basis,
    right_basis,
    first_moment,
    second_moment,
    omega_left,
    omega_right,
    sketch_left,
    sketch_right,
):
    contract_rows = (((0,), (0,)), ((), ()))
    contract_cols = (((1,), (1,)), ((), ()))
    count_dp = lax.axis_size("dp")
    own_grad = gradients[0]
    basis_rows = lax.all_gather(left_basis, "col", axis=0, tiled=True)
    piece = lax.all_gather(own_grad, "row", axis=0, tiled=True)
    rotated_part = lax.dot_general(
        basis_rows, piece, contract_rows, preferred_element_type=jnp.float32
    )
    probe_part = lax.dot_general(
        piece, omega_left, contract_rows, preferred_element_type=jnp.float32
    )
    shared = lax.psum_scatter(
        rotated_part.astype(jnp.bfloat16), "dp", scatter_dimension=0, tiled=True
    ).astype(jnp.float32)
    mean_rows = (shared / count_dp).astype(jnp.bfloat16)
    rotated_left = lax.all_gather(mean_rows, ("row", "dp"), axis=0, tiled=True)
    block_rows = rotated_left
    rotated = lax.psum_scatter(
        jnp.dot(block_rows, right_basis, preferred_element_type=jnp.float32).astype(jnp.bfloat16),
        "col",
        scatter_dimension=0,
        tiled=True,
    ).astype(jnp.float32)
    first_new = 0.9 * first_moment + 0.1 * rotated
    second_new = 0.95 * second_moment + 0.05 * rotated * rotated
    direction = (first_new / (jnp.sqrt(second_new) + 1e-08)).astype(jnp.bfloat16)
    back_terms = lax.dot_general(
        lax.all_gather(direction, "col", axis=0, tiled=True),
        right_basis,
        contract_cols,
        preferred_element_type=jnp.float32,
    )
    back_rotated = lax.psum_scatter(
        back_terms.astype(jnp.bfloat16), ("row", "dp"), scatter_dimension=0, tiled=True
    )
    band = back_rotated.shape[0]
    basis_mine = lax.dynamic_slice_in_dim(basis_rows, lax.axis_index("dp") * band, band, 1)
    block_rows = basis_mine
    update = lax.psum_scatter(
        jnp.dot(block_rows, back_rotated, preferred_element_type=jnp.float32).astype(jnp.bfloat16),
        ("row", "dp"),
        scatter_dimension=0,
        tiled=True,
    )
    probe_left = probe_part.astype(jnp.bfloat16)
    left_terms = jnp.dot(own_grad, probe_left, preferred_element_type=jnp.float32)
    right_terms = jnp.dot(own_grad, omega_right, preferred_element_type=jnp.float32)
    left_sum = lax.psum_scatter(
        left_terms.astype(jnp.bfloat16), ("col", "dp"), scatter_dimension=0, tiled=True
    ).astype(jnp.float32)
    probe_sum = lax.psum(right_terms.astype(jnp.bfloat16), "col")
    right_terms_back = lax.dot_general(
        own_grad, probe_sum, contract_rows, preferred_element_type=jnp.float32
    )
    right_sum = lax.psum(right_terms_back.astype(jnp.bfloat16), ("row", "dp")).astype(jnp.float32)
    left_new = 0.5 * sketch_left + 0.5 * left_sum / (count_dp * math.sqrt(F))
    right_new = 0.5 * sketch_right + 0.5 * right_sum / (count_dp * math.sqrt(D))
    return (update, first_new, second_new, left_new, right_new)


def solution(mesh):
    return jax.shard_map(
        on_device,
        mesh=mesh,
        in_specs=(
            P("dp", "row", "col"),
            P("col", "row"),
            P("col", ("row", "dp")),
            P("col", ("row", "dp")),
            P("col", ("row", "dp")),
            P(),
            P("col", None),
            P(("row", "col", "dp"), None),
            P("col", None),
        ),
        out_specs=(
            P(("row", "dp"), "col"),
            P("col", ("row", "dp")),
            P("col", ("row", "dp")),
            P(("row", "col", "dp"), None),
            P("col", None),
        ),
        check_vma=False,
    )
```

profile of v0, /device:TPU:6, one launch (start us, length us, event | category | flops | bytes accessed | tf_op | source)
XLA Modules:
  0.0 875.7 jit_solution(15380664746338134996)
XLA Ops:
  8.7 39.3 %all-gather.6.cloned.1.call-done = bf16[2560,640]{1,0:T(8,128)(2,1)} async-done(((bf16[160,640]{1,0:T(8,128)(2,1)}), bf16[2560,640]{1,0:T(8,128)(2,1)}) %all-gather.6.cloned.1.call-update) | async-done | bytes 3276816 | tf_op jit(solution)/shard_map/all_gather | solution.py:27
  48.0 51.5 %all-gather.12.cloned.1.call-done = bf16[1,2560,896]{2,1,0:T(8,128)(2,1)} async-done(((bf16[1,640,896]{2,1,0:T(8,128)(2,1)}), bf16[1,2560,896]{2,1,0:T(8,128)(2,1)}) %all-gather.12.cloned.1.call-update) | async-done | bytes 4587536 | tf_op jit(solution)/shard_map/all_gather | solution.py:28
  99.5 7.9 fusion.5
  107.5 27.8 %reduce-scatter.6.cloned.1.call-done = bf16[320,896]{1,0:T(8,128)(2,1)} async-done(((bf16[640,896]{1,0:T(8,128)(2,1)}), bf16[320,896]{1,0:T(8,128)(2,1)}) %reduce-scatter.6.cloned.1.call-update) | async-done | bytes 573456 | tf_op jit(solution)/shard_map/reduce_scatter | solution.py:35
  135.3 2.0 multiply_convert_fusion
  137.3 72.9 %all-gather.8.cloned.1.call-done = bf16[2560,896]{1,0:T(8,128)(2,1)} async-done(((bf16[320,896]{1,0:T(8,128)(2,1)}), bf16[2560,896]{1,0:T(8,128)(2,1)}) %all-gather.8.cloned.1.call-update) | async-done | bytes 4587536 | tf_op jit(solution)/shard_map/all_gather | solution.py:39
  210.3 13.6 %convolution_convert_fusion = bf16[2560,1792]{1,0:T(8,128)(2,1)} fusion(bf16[2560,896]{1,0:T(8,128)(2,1)} %all-gather.8.cloned.1.call-done, bf16[896,1792]{1,0:T(8,128)(2,1)S(1)} %copy-done), kind=kOutput, calls=%fused_computation | convolution fusion | flops 8225423360 | bytes 16973824 | tf_op jit(solution)/shard_map/dot_general | solution.py:42
  224.0 101.7 %reduce-scatter.8.cloned.1.call-done = bf16[160,1792]{1,0:T(8,128)(2,1)} async-done(((bf16[2560,1792]{1,0:T(8,128)(2,1)}), bf16[160,1792]{1,0:T(8,128)(2,1)}) %reduce-scatter.8.cloned.1.call-update) | async-done | bytes 573456 | tf_op jit(solution)/shard_map/reduce_scatter | solution.py:41
  325.7 3.7 divide_convert_fusion
  329.4 2.4 convolution_convert_fusion.4
  331.9 57.5 %all-gather.10.cloned.1.call-done = bf16[2560,1792]{1,0:T(8,128)(2,1)} async-done(((bf16[160,1792]{1,0:T(8,128)(2,1)}), bf16[2560,1792]{1,0:T(8,128)(2,1)}) %all-gather.10.cloned.1.call-update) | async-done | bytes 9175056 | tf_op jit(solution)/shard_map/all_gather | solution.py:51
  389.4 13.6 %convolution_convert_fusion.2 = bf16[2560,896]{1,0:T(8,128)(2,1)} fusion(bf16[2560,1792]{1,0:T(8,128)(2,1)} %all-gather.10.cloned.1.call-done, bf16[896,1792]{1,0:T(8,128)(2,1)S(1)} %copy-done), kind=kOutput, calls=%fused_computation.2 | convolution fusion | flops 8223129600 | bytes 16973824 | tf_op jit(solution)/shard_map/dot_general | solution.py:50
  403.3 97.8 %all-reduce.5.cloned.1.call-done = bf16[640,128]{1,0:T(8,128)(2,1)} async-done(((bf16[640,128]{1,0:T(8,128)(2,1)}), bf16[640,128]{1,0:T(8,128)(2,1)}) %all-reduce.5.cloned.1.call-update) | async-done | bytes 163856 | tf_op jit(solution)/shard_map/psum | solution.py:74
  501.0 2.5 fusion.11
  503.6 5.7 fusion.17
  509.4 82.9 %reduce-scatter.10.cloned.1.call-done = bf16[320,896]{1,0:T(8,128)(2,1)} async-done(((bf16[2560,896]{1,0:T(8,128)(2,1)}), bf16[320,896]{1,0:T(8,128)(2,1)}) %reduce-scatter.10.cloned.1.call-update) | async-done | bytes 573456 | tf_op jit(solution)/shard_map/reduce_scatter | solution.py:56
  592.3 6.7 convolution_convert_fusion.1
  599.8 2.0 copy.19
  603.0 72.6 %all-reduce.7.cloned.1.call-done = bf16[896,128]{0,1:T(8,128)(2,1)} async-done(((bf16[896,128]{0,1:T(8,128)(2,1)}), bf16[896,128]{0,1:T(8,128)(2,1)}) %all-reduce.7.cloned.1.call-update) | async-done | bytes 229392 | tf_op jit(solution)/shard_map/psum | solution.py:78
  675.7 2.0 multiply_add_fusion
  677.6 2.0 copy.21
  679.6 97.0 %all-reduce.9.cloned.1.call-done = bf16[640,128]{0,1:T(8,128)(2,1)} async-done(((bf16[640,128]{0,1:T(8,128)(2,1)}), bf16[640,128]{0,1:T(8,128)(2,1)}) %all-reduce.9.cloned.1.call-update) | async-done | bytes 163856
  776.6 0.9 multiply_add_fusion.1
  778.2 91.0 %reduce-scatter.12.cloned.1.call-done = bf16[320,896]{1,0:T(8,128)(2,1)} async-done(((bf16[2560,896]{1,0:T(8,128)(2,1)}), bf16[320,896]{1,0:T(8,128)(2,1)}) %reduce-scatter.12.cloned.1.call-update) | async-done | bytes 573456 | tf_op jit(solution)/shard_map/reduce_scatter | solution.py:62
  (33 shorter events, 4.2 us)
Async XLA Ops:
  7.2 203.1 %copy-start = (bf16[896,1792]{1,0:T(8,128)(2,1)S(1)}, bf16[896,1792]{1,0:T(8,128)(2,1)}, u32[]{:S(2)}) copy-start(bf16[896,1792]{1,0:T(8,128)(2,1)} %param.11) | copy-start | bytes 9633796
  7.2 40.8 %all-gather.6.cloned.1.call-start = ((), (), s32[]{:S(2)}) async-start(), calls=%async_computation.4 | async-start | bytes 3481600 | tf_op jit(solution)/shard_map/all_gather | solution.py:27
  7.9 91.6 %all-gather.12.cloned.1.call-start = ((), (), s32[]{:S(2)}) async-start(), calls=%async_computation.13 | async-start | bytes 5734400 | tf_op jit(solution)/shard_map/all_gather | solution.py:28
  8.7 126.6 %reduce-scatter.6.cloned.1.call-start = ((), (), s32[]{:S(2)}) async-start(), calls=%async_computation.5 | async-start | bytes 1720320 | tf_op jit(solution)/shard_map/reduce_scatter | solution.py:35
  107.4 102.8 %all-gather.8.cloned.1.call-start = ((), (), s32[]{:S(2)}) async-start(), calls=%async_computation.6 | async-start | bytes 5160960 | tf_op jit(solution)/shard_map/all_gather | solution.py:39
  137.3 188.4 %reduce-scatter.8.cloned.1.call-start = ((), (), s32[]{:S(2)}) async-start(), calls=%async_computation.7 | async-start | bytes 9748480 | tf_op jit(solution)/shard_map/reduce_scatter | solution.py:41
  223.9 105.5 %copy-start.1 = (bf16[896,128]{1,0:T(8,128)(2,1)S(1)}, bf16[896,128]{1,0:T(8,128)(2,1)}, u32[]{:S(2)}) copy-start(bf16[896,128]{1,0:T(8,128)(2,1)} %param.15) | copy-start | bytes 688132
  223.9 165.4 %all-gather.10.cloned.1.call-start = ((), (), s32[]{:S(2)}) async-start(), calls=%async_computation.8 | async-start | bytes 9748480 | tf_op jit(solution)/shard_map/all_gather | solution.py:51
  329.4 171.6 %all-reduce.5.cloned.1.call-start = ((), (), s32[]{:S(2)}) async-start(), calls=%async_computation.11 | async-start | bytes 327680 | tf_op jit(solution)/shard_map/psum | solution.py:74
  331.9 260.4 %reduce-scatter.10.cloned.1.call-start = ((), (), s32[]{:S(2)}) async-start(), calls=%async_computation.9 | async-start | bytes 5160960 | tf_op jit(solution)/shard_map/reduce_scatter | solution.py:56
  403.0 272.6 %all-reduce.7.cloned.1.call-start = ((), (), s32[]{:S(2)}) async-start(), calls=%async_computation.12 | async-start | bytes 458752 | tf_op jit(solution)/shard_map/psum | solution.py:78
  503.5 273.1 %all-reduce.9.cloned.1.call-start = ((), (), s32[]{:S(2)}) async-start(), calls=%async_computation.14 | async-start | bytes 327680
  509.3 359.8 %reduce-scatter.12.cloned.1.call-start = ((), (), s32[]{:S(2)}) async-start(), calls=%async_computation.10 | async-start | bytes 5160960 | tf_op jit(solution)/shard_map/reduce_scatter | solution.py:62
  599.0 0.7 copy-start.2
  599.0 2.8 copy-start.3
Sparse Core Ops, SparseCore 0:
  9.7 38.2 all-gather.5
  49.7 49.7 all-gather.11
  107.6 27.7 reduce-scatter.5
  138.0 72.1 all-gather.7
  224.0 101.6 reduce-scatter.7
  329.5 59.8 all-gather.9
  392.6 108.4 all-reduce.4
  505.0 87.2 reduce-scatter.9
  594.9 80.7 all-reduce.6
  678.8 97.7 all-reduce.8
  781.6 87.4 reduce-scatter.11
where the time goes:
time: 877 us; the launch traced here: 876 us
  waiting for transfers between devices  793 us (90%)
  matrix products  52.4 us (6%)
  between operations  14.6 us (2%)
    reduce_scatter x1, waiting for transfers between devices, on_device(): lax.psum_scatter(jnp.dot(block_rows, right_basis, preferred_element_type=...  102 us
    unnamed x12, waiting for transfers between devices  98.5 us
    psum x1, waiting for transfers between devices, on_device(): probe_sum = lax.psum(right_terms.astype(jnp.bfloat16), 'col')  97.8 us
    reduce_scatter x1, waiting for transfers between devices, on_device(): lax.psum_scatter(jnp.dot(block_rows, back_rotated, preferred_element_type...  91 us
    reduce_scatter x1, waiting for transfers between devices, on_device(): lax.psum_scatter(back_terms.astype(jnp.bfloat16), ('row', 'dp'), scatter_...  82.9 us
    all_gather x1, waiting for transfers between devices, on_device(): rotated_left = lax.all_gather(mean_rows, ('row', 'dp'), axis=0, tiled=True)  72.9 us
    psum x1, waiting for transfers between devices, on_device(): lax.psum(right_terms_back.astype(jnp.bfloat16), ('row', 'dp'))  72.6 us
    all_gather x1, waiting for transfers between devices, on_device(): lax.all_gather(direction, 'col', axis=0, tiled=True)  57.5 us
  transfers between devices with their start and end apart: 11, of which 11 were waited for; matrix products, arithmetic and copies ran while one was open for 4% of the time, Pallas kernels for 0%

commit v1 on v0

v1 whole, which is shorter than its diff:
```python
import math

import jax
import jax.numpy as jnp
from jax import lax
from jax.sharding import PartitionSpec as P

CHUNKS = 2
BF16 = jnp.bfloat16
F32 = jnp.float32


def dot(a, b, dims=((1,), (0,))):
    return lax.dot_general(a, b, (dims, ((), ())), preferred_element_type=F32)


def move(x, axis, target):
    n = lax.axis_size(axis)
    return lax.ppermute(x, axis, [(i, target(i) % n) for i in range(n)])


def on_device(
    gradients,
    left_basis,
    right_basis,
    first_moment,
    second_moment,
    omega_left,
    omega_right,
    sketch_left,
    sketch_right,
):
    n_row, n_col, n_dp = lax.axis_size("row"), lax.axis_size("col"), lax.axis_size("dp")
    row, col, dp = lax.axis_index("row"), lax.axis_index("col"), lax.axis_index("dp")
    y, z_lo, core = col // 4, (col // 2) % 2, col % 2
    n_y = n_col // 4
    own_grad = gradients[0]
    slab, width = own_grad.shape
    rows = slab * n_row
    k_dim = omega_left.shape[1]
    share = rows // n_col
    step = share // CHUNKS
    span = right_basis.shape[1]

    def swap_dp(x):
        return move(x, "dp", lambda i: i ^ 1)

    def swap_core(x):
        return move(x, "col", lambda i: i ^ 1)

    def swap_z(x):
        return move(x, "col", lambda i: i ^ 2)

    def to_row(x, s):
        return move(x, "row", lambda i: i + s)

    def to_y(x, s):
        return move(x, "col", lambda i: i + 4 * s)

    basis_wide = lax.all_gather(left_basis, "row", axis=1, tiled=True)
    by_chunk = basis_wide.reshape(share, n_col, CHUNKS, step).transpose(2, 0, 1, 3)
    basis = [
        lax.all_gather(by_chunk[k].reshape(share, n_col * step), "col", axis=0, tiled=True)
        for k in range(CHUNKS)
    ]

    omega_rows = lax.dynamic_slice_in_dim(omega_left, row * slab, slab, 0)
    probe_part = dot(omega_rows, own_grad, ((0,), (0,))).astype(BF16)
    half = slab // 2
    total = jnp.zeros((rows, width), BF16)
    probe_left_t = probe_part.astype(F32)
    for h in range(2):
        mine = own_grad[h * half : (h + 1) * half]
        summed = (mine.astype(F32) + swap_dp(mine).astype(F32)).astype(BF16)
        sent = summed if h == 0 else jnp.concatenate([summed, probe_part], 0)
        total = lax.dynamic_update_slice_in_dim(total, summed, row * slab + h * half, 0)
        for s in (1, 3, 2):
            got = to_row(sent, s)
            source = (row + n_row - s) % n_row
            total = lax.dynamic_update_slice_in_dim(
                total, got[:half], source * slab + h * half, 0
            )
            if h == 1:
                probe_left_t = probe_left_t + got[half:].astype(F32)
    probe_left_t = probe_left_t.astype(BF16)
    left_terms = dot(own_grad, probe_left_t, ((1,), (1,)))
    right_terms = dot(own_grad, omega_right)
    part = slab // n_col
    sketch_terms = jnp.concatenate(
        [right_terms.reshape(n_col, part, k_dim), left_terms.reshape(n_col, part, k_dim)], 1
    )

    def halves(x, index):
        x = x.reshape(n_col // 2, 2, x.shape[0] // n_col, x.shape[1])
        return lax.dynamic_index_in_dim(x, index, 1, keepdims=False)

    first_parts, second_parts, backs = [], [], []
    for k in range(CHUNKS):
        rotated_left = (0.5 * dot(basis[k], total, ((0,), (0,)))).astype(BF16)

        def products(index):
            block = halves(rotated_left, index)
            out = dot(block.reshape(-1, width), right_basis).reshape(n_col // 2, step, span)
            if k == 0:
                extra = lax.dynamic_index_in_dim(
                    sketch_terms.reshape(n_col // 2, 2, 2 * part, k_dim), index, 1, keepdims=False
                )
                extra = extra.reshape(n_col // 2, step, -1)
                out = jnp.concatenate([out, extra], 2)
            return out

        theirs = swap_core(products(1 - core).astype(BF16))
        pair = (products(core) + theirs.astype(F32)).astype(BF16)
        pair = pair.reshape(n_y, 2, step, -1)
        column = lax.dynamic_index_in_dim(pair, y, 0, keepdims=False).astype(F32)
        for s in (1, 3, 2):
            sent = lax.dynamic_index_in_dim(pair, (y + s) % n_y, 0, keepdims=False)
            column = column + to_y(sent, s).astype(F32)
        sent = lax.dynamic_index_in_dim(column, 1 - z_lo, 0, keepdims=False).astype(BF16)
        own = lax.dynamic_index_in_dim(column, z_lo, 0, keepdims=False)
        own = own + swap_z(sent).astype(F32)
        rotated = own[:, :span]
        lower = k * step
        first_new = 0.9 * first_moment[lower : lower + step] + 0.1 * rotated
        second_new = 0.95 * second_moment[lower : lower + step] + 0.05 * rotated * rotated
        direction = (first_new / (jnp.sqrt(second_new) + 1e-08)).astype(BF16)
        first_parts.append(first_new)
        second_parts.append(second_new)
        if k == 0:
            sketch_sum = own[:, span:].reshape(2 * part, k_dim)
        gathered = lax.all_gather(direction, "col", axis=0, tiled=True)
        backs.append(dot(gathered, right_basis, ((1,), (1,))).astype(BF16))
        if k == 0:
            probe_sum = lax.all_gather(
                sketch_sum[:part].astype(BF16), "col", axis=0, tiled=True
            )

    lines = part // n_dp
    left_mine = lax.dynamic_slice_in_dim(sketch_sum, part + dp * lines, lines, 0)
    left_sent = lax.dynamic_slice_in_dim(sketch_sum, part + (1 - dp) * lines, lines, 0)
    left_sum = left_mine + swap_dp(left_sent.astype(BF16)).astype(F32)
    f_dim = width * n_col
    left_new = 0.5 * sketch_left + 0.5 * left_sum / (n_dp * math.sqrt(f_dim))

    right_part = dot(own_grad, probe_sum, ((0,), (0,)))
    right_sent = right_part.astype(BF16)
    for s in (1, 3, 2):
        right_part = right_part + to_row(right_sent, s).astype(F32)
    right_sum = right_part.astype(BF16).astype(F32) + swap_dp(right_part.astype(BF16)).astype(F32)
    right_new = 0.5 * sketch_right + 0.5 * right_sum / (n_dp * math.sqrt(rows))

    def update_part(index):
        out = 0.0
        for k in range(CHUNKS):
            block = lax.dynamic_slice_in_dim(basis[k], index * slab, slab, 0)
            out = out + dot(block, backs[k])
        return out.astype(BF16).reshape(n_dp, 2, slab // 4, width)

    parts = {s: update_part((row + s) % n_row) for s in (1, 3, 2, 0)}
    update = []
    for h in range(2):
        acc = parts[0][:, h].astype(F32)
        for s in (1, 3, 2):
            acc = acc + to_row(parts[s][:, h], s).astype(F32)
        sent = lax.dynamic_index_in_dim(acc, 1 - dp, 0, keepdims=False).astype(BF16)
        own = lax.dynamic_index_in_dim(acc, dp, 0, keepdims=False)
        update.append((own + swap_dp(sent).astype(F32)).astype(BF16))
    return (
        jnp.concatenate(update, 0),
        jnp.concatenate(first_parts, 0),
        jnp.concatenate(second_parts, 0),
        left_new,
        right_new,
    )


def solution(mesh):
    return jax.shard_map(
        on_device,
        mesh=mesh,
        in_specs=(
            P("dp", "row", "col"),
            P("col", "row"),
            P("col", ("row", "dp")),
            P("col", ("row", "dp")),
            P("col", ("row", "dp")),
            P(),
            P("col", None),
            P(("row", "col", "dp"), None),
            P("col", None),
        ),
        out_specs=(
            P(("row", "dp"), "col"),
            P("col", ("row", "dp")),
            P("col", ("row", "dp")),
            P(("row", "col", "dp"), None),
            P("col", None),
        ),
        check_vma=False,
    )
```

time: 877 us -> 441 us (0.50)
  waiting for transfers between devices: 793 us -> 189 us
  starting transfers between devices: 0.63 us -> 50.3 us
  local copies, waits for them, and re-layouts: 6.03 us -> 45.3 us
  blocking collectives: 0 us -> 31.5 us
  matrix products: 52.4 us -> 83.5 us
  other arithmetic: 8.54 us -> 21.1 us
    reduce_scatter x4 -> x0, waiting for transfers between devices: 303 us -> none  [the longest x1 102 us: on_device(): lax.psum_scatter(jnp.dot(block_rows, right_basis, preferred_element_type=...]
    all_gather x4, waiting for transfers between devices: 221 us -> 31.5 us  [the longest x2 31.5 us: on_device(): gathered = lax.all_gather(direction, 'col', axis=0, tiled=True)]
    psum x2 -> x0, waiting for transfers between devices: 170 us -> none  [the longest x1 97.8 us: on_device(): probe_sum = lax.psum(right_terms.astype(jnp.bfloat16), 'col')]
    ppermute x0 -> x31, waiting for transfers between devices: none -> 156 us  [move(): return lax.ppermute(x, axis, [(i, target(i) % n) for i in range(n)])]
    unnamed x12 -> x4, waiting for transfers between devices: 98.5 us -> 0.57 us
    ppermute x0 -> x31, starting transfers between devices: none -> 50.2 us  [move(): return lax.ppermute(x, axis, [(i, target(i) % n) for i in range(n)])]
    all_gather x0 -> x2, blocking collectives: none -> 31.5 us  [the longest x1 16.9 us: on_device(): lax.all_gather(sketch_sum[:part].astype(BF16), 'col', axis=0, tiled=True)]
    dot_general x7 -> x20, matrix products: 52.4 us -> 83.5 us  [dot(): return lax.dot_general(a, b, (dims, ((), ())), preferred_element_type=F32)]
  transfers between devices with their start and end apart: 11 -> 35, of which waited for: 11 -> 20; matrix products, arithmetic and copies ran while one was open for 4% -> 28% of each run, Pallas kernels for 0% -> 0%
where the time goes in v1:
time: 441 us; the launch traced here: 435 us
  waiting for transfers between devices  189 us (43%)
  matrix products  83.5 us (19%)
  starting transfers between devices  50.3 us (11%)
  local copies, waits for them, and re-layouts  45.3 us (10%)
  blocking collectives  31.5 us (7%)
  other arithmetic  21.1 us (5%)
  between operations  14.4 us (3%)
    ppermute x31, waiting for transfers between devices, move(): return lax.ppermute(x, axis, [(i, target(i) % n) for i in range(n)])  156 us
    dot_general x20, matrix products, dot(): return lax.dot_general(a, b, (dims, ((), ())), preferred_element_type=F32)  83.5 us
    ppermute x31, starting transfers between devices, move(): return lax.ppermute(x, axis, [(i, target(i) % n) for i in range(n)])  50.2 us
    all_gather x2, waiting for transfers between devices, on_device(): gathered = lax.all_gather(direction, 'col', axis=0, tiled=True)  31.5 us
    all_gather x1, blocking collectives, on_device(): lax.all_gather(sketch_sum[:part].astype(BF16), 'col', axis=0, tiled=True)  16.9 us
    all_gather x1, blocking collectives, on_device(): basis_wide = lax.all_gather(left_basis, 'row', axis=1, tiled=True)  14.6 us
    dynamic_update_slice x6, local copies, waits for them, and re-layouts, on_device(): lax.dynamic_update_slice_in_dim(total, got[:half], source * slab + h * ha...  11.5 us
  transfers between devices with their start and end apart: 35, of which 20 were waited for; matrix products, arithmetic and copies ran while one was open for 28% of the time, Pallas kernels for 0%

profile of v1, /device:TPU:6, one launch (start us, length us, event | category | flops | bytes accessed | tf_op | source)
XLA Modules:
  0.0 434.6 jit_solution(7215370016764518020)
XLA Ops:
  7.2 14.6 %all_gather.18 = bf16[160,2560]{1,0:T(8,128)(2,1)} all-gather(bf16[160,640]{1,0:T(8,128)(2,1)} %param.10), channel_id=1, replica_groups=mesh['row'=4,'col'=16,'dp'=2] {'row'}, dimensions={1}, use_global_device_ids=true | all-gather | bytes 1024000 | tf_op jit(solution)/shard_map/all_gather | solution.py:60
  39.3 20.4 %collective-permute-done = bf16[320,896]{1,0:T(8,128)(2,1)} collective-permute-done((bf16[320,896]{1,0:T(8,128)(2,1)}, bf16[320,896]{1,0:T(8,128)(2,1)}, u32[]{:S(2)}, u32[]{:S(2)}) %collective-permute-start) | collective-permute-done | bytes 573472 | tf_op jit(solution)/shard_map/ppermute | solution.py:19
  64.3 4.5 %collective-permute-start.1 = (bf16[320,896]{1,0:T(8,128)(2,1)}, bf16[320,896]{1,0:T(8,128)(2,1)}, u32[]{:S(2)}, u32[]{:S(2)}) collective-permute-start(bf16[320,896]{1,0:T(8,128)(2,1)} %get-tuple-element.24), channel_id=1, source_target_pairs={{0,32},{32,64},{64,96},{96,0},{1,33},{33,65},{65,97},{97,1},{2,34}... | collective-permute-start | bytes 1720328 | tf_op jit(solution)/shard_map/ppermute | solution.py:19
  76.0 7.5 %collective-permute-done.1 = bf16[320,896]{1,0:T(8,128)(2,1)} collective-permute-done((bf16[320,896]{1,0:T(8,128)(2,1)}, bf16[320,896]{1,0:T(8,128)(2,1)}, u32[]{:S(2)}, u32[]{:S(2)}) %collective-permute-start.1) | collective-permute-done | bytes 573472 | tf_op jit(solution)/shard_map/ppermute | solution.py:19
  103.7 22.0 %collective-permute-done.5 = bf16[448,896]{1,0:T(8,128)(2,1)} collective-permute-done((bf16[448,896]{1,0:T(8,128)(2,1)}, bf16[448,896]{1,0:T(8,128)(2,1)}, u32[]{:S(2)}, u32[]{:S(2)}) %collective-permute-start.5) | collective-permute-done | bytes 802848 | tf_op jit(solution)/shard_map/ppermute | solution.py:19
  139.6 11.8 %fusion.15 = bf16[1280,896]{0,1:T(8,128)(2,1)} fusion(bf16[2560,896]{1,0:T(8,128)(2,1)} %slice_dynamic-update-slice_fusion, bf16[2560,1280]{1,0:T(8,128)(2,1)} %all-gather.5.cloned.1.call-done), kind=kOutput, calls=%fused_computation.17 | convolution fusion | flops 5874319360 | bytes 13434880 | tf_op jit(solution)/shard_map/dot_general | solution.py:14
  151.5 4.4 %copy.30 = bf16[1280,896]{1,0:T(8,128)(2,1)} copy(bf16[1280,896]{0,1:T(8,128)(2,1)} %fusion.15) | data formatting | bytes 4587520 | tf_op jit(solution)/shard_map/convert_element_type | solution.py:99
  161.5 11.8 %fusion.16 = bf16[1280,896]{0,1:T(8,128)(2,1)} fusion(bf16[2560,896]{1,0:T(8,128)(2,1)} %slice_dynamic-update-slice_fusion, bf16[2560,1280]{1,0:T(8,128)(2,1)} %all-gather.9.cloned.1.call-done), kind=kOutput, calls=%fused_computation.18 | convolution fusion | flops 5874319360 | bytes 13434880 | tf_op jit(solution)/shard_map/dot_general | solution.py:14
  173.3 4.3 copy.34
  177.6 5.2 %fusion.12 = bf16[8,80,1792]{2,1,0:T(8,128)(2,1)} fusion(bf16[896,1792]{1,0:T(8,128)(2,1)S(1)} %copy-done, bf16[8,2,80,896]{3,2,1,0:T(8,128)(2,1)} %bitcast.183, s32[]{:T(128)S(6)} %select_n.169), kind=kOutput, calls=%fused_computation.16 | convolution fusion | flops 2056355840 | bytes 6651908 | tf_op jit(solution)/shard_map/dot_general | solution.py:14
  195.2 4.2 add_convert_fusion
  202.8 18.6 %collective-permute-done.10 = bf16[2,80,1920]{2,1,0:T(8,128)(2,1)S(1)} collective-permute-done((bf16[2,80,1920]{2,1,0:T(8,128)(2,1)S(1)}, bf16[2,80,1920]{2,1,0:T(8,128)(2,1)S(1)}, u32[]{:S(2)}, u32[]{:S(2)}) %collective-permute-start.10) | collective-permute-done | bytes 614432 | tf_op jit(solution)/shard_map/ppermute | solution.py:19
  224.8 12.7 %collective-permute-done.14 = bf16[2,80,1792]{2,1,0:T(8,128)(2,1)S(1)} collective-permute-done((bf16[2,80,1792]{2,1,0:T(8,128)(2,1)S(1)}, bf16[2,80,1792]{2,1,0:T(8,128)(2,1)S(1)}, u32[]{:S(2)}, u32[]{:S(2)}) %collective-permute-start.14) | collective-permute-done | bytes 573472 | tf_op jit(solution)/shard_map/ppermute | solution.py:19
  237.4 7.6 %collective-permute-done.15 = bf16[2,80,1792]{2,1,0:T(8,128)(2,1)S(1)} collective-permute-done((bf16[2,80,1792]{2,1,0:T(8,128)(2,1)S(1)}, bf16[2,80,1792]{2,1,0:T(8,128)(2,1)S(1)}, u32[]{:S(2)}, u32[]{:S(2)}) %collective-permute-start.15) | collective-permute-done | bytes 573472 | tf_op jit(solution)/shard_map/ppermute | solution.py:19
  249.4 7.6 %collective-permute-done.17 = bf16[80,1792]{1,0:T(8,128)(2,1)S(1)} collective-permute-done((bf16[80,1792]{1,0:T(8,128)(2,1)S(1)}, bf16[80,1792]{1,0:T(8,128)(2,1)S(1)}, u32[]{:S(2)}, u32[]{:S(2)}) %collective-permute-start.17) | collective-permute-done | bytes 286752 | tf_op jit(solution)/shard_map/ppermute | solution.py:19
  262.4 16.9 %all_gather.23 = bf16[640,128]{1,0:T(8,128)(2,1)S(1)} all-gather(bf16[40,128]{1,0:T(8,128)(2,1)S(1)} %slice.169), channel_id=1, replica_groups=mesh['row'=4,'col'=16,'dp'=2] {'col'}, dimensions={0}, use_global_device_ids=true | all-gather | bytes 174080 | tf_op jit(solution)/shard_map/all_gather | solution.py:134
  285.2 4.2 collective-permute-start.26
  291.7 4.3 collective-permute-done.28
  296.1 8.5 %convolution_convert_fusion = bf16[1280,896]{1,0:T(8,128)(2,1)} fusion(bf16[1280,1792]{1,0:T(8,128)(2,1)} %all-gather.11.cloned.1.call-done, bf16[896,1792]{1,0:T(8,128)(2,1)S(1)} %copy-done), kind=kOutput, calls=%fused_computation.5 | convolution fusion | flops 4111564800 | bytes 10092544 | tf_op jit(solution)/shard_map/dot_general | solution.py:14
  304.6 31.5 %all-gather.7.cloned.1.call-done = bf16[1280,1792]{1,0:T(8,128)(2,1)} async-done(((bf16[80,1792]{1,0:T(8,128)(2,1)}), bf16[1280,1792]{1,0:T(8,128)(2,1)}) %all-gather.7.cloned.1.call-update) | async-done | bytes 4587536 | tf_op jit(solution)/shard_map/all_gather | solution.py:131
  336.1 7.4 %convolution_convert_fusion.1 = bf16[1280,896]{1,0:T(8,128)(2,1)S(1)} fusion(bf16[1280,1792]{1,0:T(8,128)(2,1)} %all-gather.7.cloned.1.call-done, bf16[896,1792]{1,0:T(8,128)(2,1)S(1)} %copy-done), kind=kOutput, calls=%fused_computation.6 | convolution fusion | flops 4111564800 | bytes 10092544 | tf_op jit(solution)/shard_map/dot_general | solution.py:14
  371.6 7.1 %collective-permute-done.22 = bf16[2,160,896]{2,1,0:T(8,128)(2,1)S(1)} collective-permute-done((bf16[2,160,896]{2,1,0:T(8,128)(2,1)S(1)}, bf16[2,160,896]{2,1,0:T(8,128)(2,1)S(1)}, u32[]{:S(2)}, u32[]{:S(2)}) %collective-permute-start.22) | collective-permute-done | bytes 573472 | tf_op jit(solution)/shard_map/ppermute | solution.py:19
  381.8 27.5 %collective-permute-done.23 = bf16[2,160,896]{2,1,0:T(8,128)(2,1)S(1)} collective-permute-done((bf16[2,160,896]{2,1,0:T(8,128)(2,1)S(1)}, bf16[2,160,896]{2,1,0:T(8,128)(2,1)S(1)}, u32[]{:S(2)}, u32[]{:S(2)}) %collective-permute-start.23) | collective-permute-done | bytes 573472 | tf_op jit(solution)/shard_map/ppermute | solution.py:19
  417.8 4.5 %collective-permute-done.21 = bf16[160,896]{1,0:T(8,128)(2,1)} collective-permute-done((bf16[160,896]{1,0:T(8,128)(2,1)}, bf16[160,896]{1,0:T(8,128)(2,1)}, u32[]{:S(2)}, u32[]{:S(2)}) %collective-permute-start.21) | collective-permute-done | bytes 286752 | tf_op jit(solution)/shard_map/ppermute | solution.py:19
  (167 shorter events, 151.2 us)
Async XLA Ops:
  7.2 132.5 %all-gather.5.cloned.1.call-start = ((), (), s32[]{:S(2)}) async-start(), calls=%async_computation | async-start | bytes 6963200 | tf_op jit(solution)/shard_map/all_gather | solution.py:63
  30.5 131.0 %all-gather.9.cloned.1.call-start = ((), (), s32[]{:S(2)}) async-start(), calls=%async_computation.2 | async-start | bytes 6963200 | tf_op jit(solution)/shard_map/all_gather | solution.py:63
  33.0 263.1 %all-gather.11.cloned.1.call-start = ((), (), s32[]{:S(2)}) async-start(), calls=%async_computation.3 | async-start | bytes 4874240 | tf_op jit(solution)/shard_map/all_gather | solution.py:131
  35.4 24.3 %collective-permute-start = (bf16[320,896]{1,0:T(8,128)(2,1)}, bf16[320,896]{1,0:T(8,128)(2,1)}, u32[]{:S(2)}, u32[]{:S(2)}) collective-permute-start(bf16[320,896]{1,0:T(8,128)(2,1)} %get-tuple-element.45), channel_id=1, source_target_pairs={{0,1},{1,0},{2,3},{3,2},{4,5},{5,4},{6,7},{7,6},{8,9},{9,8},{10,11... | collective-permute-start | bytes 1720328 | tf_op jit(solution)/shard_map/ppermute | solution.py:19
  68.7 20.1 %collective-permute-start.3 = (bf16[320,896]{1,0:T(8,128)(2,1)}, bf16[320,896]{1,0:T(8,128)(2,1)}, u32[]{:S(2)}, u32[]{:S(2)}) collective-permute-start(bf16[320,896]{1,0:T(8,128)(2,1)} %get-tuple-element.24), channel_id=1, source_target_pairs={{0,64},{32,96},{64,0},{96,32},{1,65},{33,97},{65,1},{97,33},{2,66}... | collective-permute-start | bytes 1720328 | tf_op jit(solution)/shard_map/ppermute | solution.py:19
  70.2 23.1 %collective-permute-start.4 = (bf16[320,896]{1,0:T(8,128)(2,1)}, bf16[320,896]{1,0:T(8,128)(2,1)}, u32[]{:S(2)}, u32[]{:S(2)}) collective-permute-start(bf16[320,896]{1,0:T(8,128)(2,1)} %get-tuple-element.44), channel_id=1, source_target_pairs={{0,1},{1,0},{2,3},{3,2},{4,5},{5,4},{6,7},{7,6},{8,9},{9,8},{10,11... | collective-permute-start | bytes 1720328 | tf_op jit(solution)/shard_map/ppermute | solution.py:19
  96.2 29.5 %collective-permute-start.5 = (bf16[448,896]{1,0:T(8,128)(2,1)}, bf16[448,896]{1,0:T(8,128)(2,1)}, u32[]{:S(2)}, u32[]{:S(2)}) collective-permute-start(bf16[448,896]{1,0:T(8,128)(2,1)} %pad_maximum_fusion.3), channel_id=1, source_target_pairs={{0,32},{32,64},{64,96},{96,0},{1,33},{33,65},{65,97},{97,1},{2,34}... | collective-permute-start | bytes 2408456 | tf_op jit(solution)/shard_map/ppermute | solution.py:19
  98.6 29.7 %collective-permute-start.6 = (bf16[448,896]{1,0:T(8,128)(2,1)}, bf16[448,896]{1,0:T(8,128)(2,1)}, u32[]{:S(2)}, u32[]{:S(2)}) collective-permute-start(bf16[448,896]{1,0:T(8,128)(2,1)} %pad_maximum_fusion.3), channel_id=1, source_target_pairs={{0,96},{32,0},{64,32},{96,64},{1,97},{33,1},{65,33},{97,65},{2,98}... | collective-permute-start | bytes 2408456 | tf_op jit(solution)/shard_map/ppermute | solution.py:19
  98.6 29.7 %collective-permute-start.7 = (bf16[448,896]{1,0:T(8,128)(2,1)}, bf16[448,896]{1,0:T(8,128)(2,1)}, u32[]{:S(2)}, u32[]{:S(2)}) collective-permute-start(bf16[448,896]{1,0:T(8,128)(2,1)} %pad_maximum_fusion.3), channel_id=1, source_target_pairs={{0,64},{32,96},{64,0},{96,32},{1,65},{33,97},{65,1},{97,33},{2,66}... | collective-permute-start | bytes 2408456 | tf_op jit(solution)/shard_map/ppermute | solution.py:19
  161.3 26.7 %collective-permute-start.8 = (bf16[8,80,1920]{2,1,0:T(8,128)(2,1)}, bf16[8,80,1920]{2,1,0:T(8,128)(2,1)}, u32[]{:S(2)}, u32[]{:S(2)}) collective-permute-start(bf16[8,80,1920]{2,1,0:T(8,128)(2,1)} %pad_maximum_fusion), channel_id=1, source_target_pairs={{0,2},{2,0},{4,6},{6,4},{8,10},{10,8},{12,14},{14,12},{16,18},{18,... | collective-permute-start | bytes 7372808 | tf_op jit(solution)/shard_map/ppermute | solution.py:19
  190.5 30.9 %collective-permute-start.10 = (bf16[2,80,1920]{2,1,0:T(8,128)(2,1)S(1)}, bf16[2,80,1920]{2,1,0:T(8,128)(2,1)S(1)}, u32[]{:S(2)}, u32[]{:S(2)}) collective-permute-start(bf16[2,80,1920]{2,1,0:T(8,128)(2,1)S(1)} %get-tuple-element.27), channel_id=1, source_target_pairs={{0,24},{2,26},{4,28},{6,30},{8,0},{10,2},{12,4},{14,6},{16,8},{18,... | collective-permute-start | bytes 1843208 | tf_op jit(solution)/shard_map/ppermute | solution.py:19
  194.0 27.4 %collective-permute-start.11 = (bf16[2,80,1920]{2,1,0:T(8,128)(2,1)S(1)}, bf16[2,80,1920]{2,1,0:T(8,128)(2,1)S(1)}, u32[]{:S(2)}, u32[]{:S(2)}) collective-permute-start(bf16[2,80,1920]{2,1,0:T(8,128)(2,1)S(1)} %get-tuple-element.26), channel_id=1, source_target_pairs={{0,16},{2,18},{4,20},{6,22},{8,24},{10,26},{12,28},{14,30},{16,0},... | collective-permute-start | bytes 1843208 | tf_op jit(solution)/shard_map/ppermute | solution.py:19
  194.0 30.3 %collective-permute-start.9 = (bf16[2,80,1920]{2,1,0:T(8,128)(2,1)S(1)}, bf16[2,80,1920]{2,1,0:T(8,128)(2,1)S(1)}, u32[]{:S(2)}, u32[]{:S(2)}) collective-permute-start(bf16[2,80,1920]{2,1,0:T(8,128)(2,1)S(1)} %get-tuple-element.25), channel_id=1, source_target_pairs={{0,8},{2,10},{4,12},{6,14},{8,16},{10,18},{12,20},{14,22},{16,24},... | collective-permute-start | bytes 1843208 | tf_op jit(solution)/shard_map/ppermute | solution.py:19
  199.5 37.9 %collective-permute-start.14 = (bf16[2,80,1792]{2,1,0:T(8,128)(2,1)S(1)}, bf16[2,80,1792]{2,1,0:T(8,128)(2,1)S(1)}, u32[]{:S(2)}, u32[]{:S(2)}) collective-permute-start(bf16[2,80,1792]{2,1,0:T(8,128)(2,1)S(1)} %get-tuple-element.31), channel_id=1, source_target_pairs={{0,8},{2,10},{4,12},{6,14},{8,16},{10,18},{12,20},{14,22},{16,24},... | collective-permute-start | bytes 1720328 | tf_op jit(solution)/shard_map/ppermute | solution.py:19
  202.1 43.0 %collective-permute-start.15 = (bf16[2,80,1792]{2,1,0:T(8,128)(2,1)S(1)}, bf16[2,80,1792]{2,1,0:T(8,128)(2,1)S(1)}, u32[]{:S(2)}, u32[]{:S(2)}) collective-permute-start(bf16[2,80,1792]{2,1,0:T(8,128)(2,1)S(1)} %get-tuple-element.33), channel_id=1, source_target_pairs={{0,24},{2,26},{4,28},{6,30},{8,0},{10,2},{12,4},{14,6},{16,8},{18,... | collective-permute-start | bytes 1720328 | tf_op jit(solution)/shard_map/ppermute | solution.py:19
  221.4 27.4 %collective-permute-start.16 = (bf16[2,80,1792]{2,1,0:T(8,128)(2,1)S(1)}, bf16[2,80,1792]{2,1,0:T(8,128)(2,1)S(1)}, u32[]{:S(2)}, u32[]{:S(2)}) collective-permute-start(bf16[2,80,1792]{2,1,0:T(8,128)(2,1)S(1)} %get-tuple-element.32), channel_id=1, source_target_pairs={{0,16},{2,18},{4,20},{6,22},{8,24},{10,26},{12,28},{14,30},{16,0},... | collective-permute-start | bytes 1720328 | tf_op jit(solution)/shard_map/ppermute | solution.py:19
  224.7 24.6 %collective-permute-start.12 = (bf16[80,1920]{1,0:T(8,128)(2,1)S(1)}, bf16[80,1920]{1,0:T(8,128)(2,1)S(1)}, u32[]{:S(2)}, u32[]{:S(2)}) collective-permute-start(bf16[80,1920]{1,0:T(8,128)(2,1)S(1)} %fusion.72), channel_id=1, source_target_pairs={{0,4},{2,6},{4,0},{6,2},{8,12},{10,14},{12,8},{14,10},{16,20},{18,... | collective-permute-start | bytes 921608 | tf_op jit(solution)/shard_map/ppermute | solution.py:19
  258.9 77.2 %all-gather.7.cloned.1.call-start = ((), (), s32[]{:S(2)}) async-start(), calls=%async_computation.1 | async-start | bytes 4874240 | tf_op jit(solution)/shard_map/all_gather | solution.py:131
  351.2 27.6 %collective-permute-start.22 = (bf16[2,160,896]{2,1,0:T(8,128)(2,1)S(1)}, bf16[2,160,896]{2,1,0:T(8,128)(2,1)S(1)}, u32[]{:S(2)}, u32[]{:S(2)}) collective-permute-start(bf16[2,160,896]{2,1,0:T(8,128)(2,1)S(1)} %get-tuple-element.39), channel_id=1, source_target_pairs={{0,32},{32,64},{64,96},{96,0},{1,33},{33,65},{65,97},{97,1},{2,34}... | collective-permute-start | bytes 1720328 | tf_op jit(solution)/shard_map/ppermute | solution.py:19
  356.5 25.2 %collective-permute-start.19 = (bf16[2,160,896]{2,1,0:T(8,128)(2,1)S(1)}, bf16[2,160,896]{2,1,0:T(8,128)(2,1)S(1)}, u32[]{:S(2)}, u32[]{:S(2)}) collective-permute-start(bf16[2,160,896]{2,1,0:T(8,128)(2,1)S(1)} %get-tuple-element.40), channel_id=1, source_target_pairs={{0,96},{32,0},{64,32},{96,64},{1,97},{33,1},{65,33},{97,65},{2,98}... | collective-permute-start | bytes 1720328 | tf_op jit(solution)/shard_map/ppermute | solution.py:19
  357.2 52.1 %collective-permute-start.23 = (bf16[2,160,896]{2,1,0:T(8,128)(2,1)S(1)}, bf16[2,160,896]{2,1,0:T(8,128)(2,1)S(1)}, u32[]{:S(2)}, u32[]{:S(2)}) collective-permute-start(bf16[2,160,896]{2,1,0:T(8,128)(2,1)S(1)} %get-tuple-element.41), channel_id=1, source_target_pairs={{0,96},{32,0},{64,32},{96,64},{1,97},{33,1},{65,33},{97,65},{2,98}... | collective-permute-start | bytes 1720328 | tf_op jit(solution)/shard_map/ppermute | solution.py:19
  362.6 46.6 %collective-permute-start.20 = (bf16[2,160,896]{2,1,0:T(8,128)(2,1)S(1)}, bf16[2,160,896]{2,1,0:T(8,128)(2,1)S(1)}, u32[]{:S(2)}, u32[]{:S(2)}) collective-permute-start(bf16[2,160,896]{2,1,0:T(8,128)(2,1)S(1)} %get-tuple-element.42), channel_id=1, source_target_pairs={{0,64},{32,96},{64,0},{96,32},{1,65},{33,97},{65,1},{97,33},{2,66}... | collective-permute-start | bytes 1720328 | tf_op jit(solution)/shard_map/ppermute | solution.py:19
  366.5 42.8 %collective-permute-start.24 = (bf16[2,160,896]{2,1,0:T(8,128)(2,1)S(1)}, bf16[2,160,896]{2,1,0:T(8,128)(2,1)S(1)}, u32[]{:S(2)}, u32[]{:S(2)}) collective-permute-start(bf16[2,160,896]{2,1,0:T(8,128)(2,1)S(1)} %get-tuple-element.43), channel_id=1, source_target_pairs={{0,64},{32,96},{64,0},{96,32},{1,65},{33,97},{65,1},{97,33},{2,66}... | collective-permute-start | bytes 1720328 | tf_op jit(solution)/shard_map/ppermute | solution.py:19
  378.7 36.2 %collective-permute-start.30 = (bf16[896,128]{0,1:T(8,128)(2,1)S(1)}, bf16[896,128]{0,1:T(8,128)(2,1)S(1)}, u32[]{:S(2)}, u32[]{:S(2)}) collective-permute-start(bf16[896,128]{0,1:T(8,128)(2,1)S(1)} %add_convert_fusion.7), channel_id=1, source_target_pairs={{0,1},{1,0},{2,3},{3,2},{4,5},{5,4},{6,7},{7,6},{8,9},{9,8},{10,11... | collective-permute-start | bytes 688136 | tf_op jit(solution)/shard_map/ppermute | solution.py:19
  (33 other events, 574.2 us)
Sparse Core Ops, SparseCore 0:
  30.6 63.1 all-gather.4
  95.5 42.7 all-gather.8
  259.0 37.0 all-gather.10
  297.6 38.4 all-gather.6
